TPU v7x, 32 devices: a whole 2x2x4 slice. The times are simulated.
32 devices in a mesh: row: 8 (over z, y), col: 4 (over x, core).
Axes of the slice: x: 2, y: 2, z: 4, core: 2. Of those that a mesh axis runs over, the one named last changes fastest.
Arguments:
- lambda_amps: float32 [32, 32768], P('col', 'row'), may hold values from -6 to 6
- cycle_inter: float32 [32768, 4096], P('row', 'col'), may hold values from -0.03125 to 0.03125
- exchanged: int32 [4096], replicated, may hold values from 0 to 4095, each once
- occ_energy: float32 [64], replicated, may hold values from -1 to -0.25
- virt_energy: float32 [512], replicated, may hold values from 0.25 to 1.5
- row_orbitals: int32 [32, 2], replicated, may hold values from 0 to 63
- col_orbitals: int32 [4096, 2], replicated, may hold values from 0 to 511
Outputs:
- update: float32 [32, 4096], P(('row', 'col'))
All inputs are finite; a program needn't handle non-finite values.
Results may differ from a plain program's by a relative error of at most 0.000088.
Values sent between devices are 32-bit elements; how exact they have to be, the bound alone decides.
A program may use at most 64 MiB of HBM per device.

v0:
```python
import jax
import jax.numpy as jnp
from jax import lax
from jax.sharding import PartitionSpec as P


def shards(
    lambda_amps, cycle_inter, exchanged, occ_energy, virt_energy, row_orbitals, col_orbitals
):
    n_row = lax.axis_size("row")
    n_col = lax.axis_size("col")
    per_owner = lambda_amps.shape[0] // n_row
    partial_value = jnp.dot(
        lax.all_gather(lambda_amps, "col", axis=0, tiled=True),
        cycle_inter,
        precision=lax.Precision.HIGHEST,
        preferred_element_type=jnp.float32,
    )
    summed = lax.psum_scatter(partial_value, "row", scatter_dimension=0, tiled=True)
    cycle = lax.all_to_all(summed, "col", split_axis=0, concat_axis=1, tiled=True)
    anti = cycle - jnp.take(cycle, exchanged, axis=1)
    first_row = (lax.axis_index("row") * n_col + lax.axis_index("col")) * per_owner
    mine = lax.dynamic_slice_in_dim(row_orbitals, first_row, per_owner, 0)
    row_part = jnp.take(occ_energy, mine[:, 0]) + jnp.take(occ_energy, mine[:, 1])
    col_part = jnp.take(virt_energy, col_orbitals[:, 0]) + jnp.take(virt_energy, col_orbitals[:, 1])
    denom = row_part[:, None] - col_part[None, :]
    return anti / denom


def solution(mesh):
    placed = (P("col", "row"), P("row", "col"), P(), P(), P(), P(), P())
    return jax.shard_map(
        shards, mesh=mesh, in_specs=placed, out_specs=P(("row", "col"), None), check_vma=False
    )
```

profile of v0, /device:TPU:0, one launch (start us, length us, event | category | flops | bytes accessed | tf_op | source)
XLA Modules:
  0.0 192.9 jit_solution(14704631461317259358)
XLA Ops:
  6.5 0.0 copy-start
  6.5 0.0 copy-start.5
  6.5 0.0 copy-start.2
  6.5 0.0 copy-start.1
  6.5 0.0 copy-start.4
  6.5 0.0 all-reduce.3.cloned.1.call-start
  6.6 9.0 %all_gather.3 = f32[32,4096]{1,0:T(8,128)S(1)} all-gather(f32[8,4096]{1,0:T(8,128)} %param.9), channel_id=1, replica_groups=mesh['row'=8,'col'=4] {'col'}, dimensions={0}, use_global_device_ids=true | all-gather | bytes 655360 | tf_op jit(solution)/shard_map/all_gather | solution.py:14
  15.6 13.8 %fusion.8 = f32[32,1024]{1,0:T(8,128)} fusion(f32[32,4096]{1,0:T(8,128)S(1)} %all_gather.3, f32[4096,1024]{1,0:T(8,128)} %param.10), kind=kOutput, calls=%fused_computation.17 | convolution fusion | flops 1610612736 | bytes 17432576 | tf_op jit(solution)/shard_map/dot_general | solution.py:13
  29.3 0.0 all-reduce.3.cloned.1.call-update
  29.3 0.0 copy-done.2
  29.4 0.0 copy-done.1
  29.4 0.0 copy-done.5
  29.5 0.6 dynamic-slice.6
  30.7 0.0 copy-done.4
  30.7 0.1 constant_dynamic-slice_fusion
  30.8 69.2 %all-reduce.3.cloned.1.call-done = f32[32,1024]{1,0:T(8,128)} async-done(((f32[32,1024]{1,0:T(8,128)}), f32[32,1024]{1,0:T(8,128)}) %all-reduce.3.cloned.1.call-update) | async-done | bytes 131088
  100.0 0.8 dynamic-slice_bitcast_fusion
  100.8 0.6 copy.8
  101.4 3.3 %all-to-all-start = ((f32[4,1,1024]{2,1,0:T(1,128)}), f32[4,1,1024]{2,1,0:T(1,128)S(1)}, u32[]{:S(2)}, u32[]{:S(2)}) async-start(f32[4,1,1024]{2,1,0:T(1,128)} %copy.8), calls=%async_computation | async-start | bytes 32768 | tf_op jit(solution)/shard_map/all_to_all | solution.py:20
  104.6 0.5 fusion.6
  108.8 0.0 copy-done
  108.8 0.0 copy-start.3
  108.8 25.8 %gather_fusion.2 = f32[4096]{0:T(1024)S(1)} fusion(f32[512]{0:T(512)S(1)} %copy-done, s32[4096]{0:T(1024)S(1)} %fusion.4), kind=kCustom, calls=%fused_computation.1.clone | custom fusion | bytes 49152 | tf_op jit(solution)/shard_map/jit(_take)/gather | solution.py:25
  134.7 25.8 %gather_fusion.1 = f32[4096]{0:T(1024)S(1)} fusion(f32[512]{0:T(512)S(1)} %copy-done, s32[4096]{0:T(1024)S(1)} %fusion.3), kind=kCustom, calls=%fused_computation.clone | custom fusion | bytes 49152 | tf_op jit(solution)/shard_map/jit(_take)/gather | solution.py:25
  160.5 0.0 copy-done.3
  160.5 0.6 fusion.7
  162.4 0.0 all-to-all-done
  162.4 23.0 %gather_fusion = f32[4096]{0:T(1024)S(1)} fusion(f32[4096]{0:T(1024)S(1)} %bitcast.14, s32[4096]{0:T(1024)S(1)} %fusion.2), kind=kCustom, calls=%fused_computation.2 | custom fusion | bytes 49152 | tf_op jit(solution)/shard_map/jit(_take)/gather | solution.py:21
  185.4 0.6 fusion.1
  (4 shorter events, 0.0 us)
Async XLA Ops:
  6.5 102.2 %copy-start = (f32[512]{0:T(512)S(1)}, f32[512]{0:T(512)}, u32[]{:S(2)}) copy-start(f32[512]{0:T(512)} %param.13) | copy-start | bytes 6148
  6.5 22.9 %copy-start.5 = (u32[32]{0:T(128)S(1)}, u32[32]{0:T(128)}, u32[]{:S(2)}) copy-start(u32[32]{0:T(128)} %constant.105) | copy-start | bytes 388
  6.5 22.8 %copy-start.2 = (s32[4096,2]{0,1:T(2,128)S(1)}, s32[4096,2]{0,1:T(2,128)}, u32[]{:S(2)}) copy-start(s32[4096,2]{0,1:T(2,128)} %param.15) | copy-start | bytes 98308
  6.5 22.9 %copy-start.1 = (s32[4096]{0:T(1024)S(1)}, s32[4096]{0:T(1024)}, u32[]{:S(2)}) copy-start(s32[4096]{0:T(1024)} %param.11) | copy-start | bytes 49156
  6.5 24.1 %copy-start.4 = (s32[32,2]{0,1:T(2,128)S(1)}, s32[32,2]{0,1:T(2,128)}, u32[]{:S(2)}) copy-start(s32[32,2]{0,1:T(2,128)} %param.14) | copy-start | bytes 772
  6.5 93.4 %all-reduce.3.cloned.1.call-start = ((), (), s32[]{:S(2)}) async-start(), calls=%async_computation.1 | async-start | bytes 262144
  101.4 61.0 %all-to-all-start = ((f32[4,1,1024]{2,1,0:T(1,128)}), f32[4,1,1024]{2,1,0:T(1,128)S(1)}, u32[]{:S(2)}, u32[]{:S(2)}) async-start(f32[4,1,1024]{2,1,0:T(1,128)} %copy.8), calls=%async_computation | async-start | bytes 32768 | tf_op jit(solution)/shard_map/all_to_all | solution.py:20
  108.8 51.7 %copy-start.3 = (f32[64]{0:T(128)S(1)}, f32[64]{0:T(128)}, u32[]{:S(2)}) copy-start(f32[64]{0:T(128)} %param.12) | copy-start | bytes 772
Sparse Core Ops, SparseCore 0:
  29.5 70.4 all-reduce.2
where the time goes:
time: 193 us
  local copies, waits for them, and re-layouts  78 us (40%)
  waiting for transfers between devices  69.2 us (36%)
  between operations  19 us (10%)
  matrix products  13.8 us (7%)
  blocking collectives  8.96 us (5%)
  starting transfers between devices  3.29 us (2%)
    unnamed x2, waiting for transfers between devices  69.2 us
    gather x1, local copies, waits for them, and re-layouts, shards(): jnp.take(virt_energy, col_orbitals[:, 0])  25.8 us
    gather x1, local copies, waits for them, and re-layouts, shards(): jnp.take(virt_energy, col_orbitals[:, 1])  25.8 us
    gather x1, local copies, waits for them, and re-layouts, shards(): anti = cycle - jnp.take(cycle, exchanged, axis=1)  23 us
    dot_general x1, matrix products, shards(): jnp.dot(lax.all_gather(lambda_amps, 'col', axis=0, tiled=True), cycle_int...  13.8 us
    all_gather x1, blocking collectives, shards(): lax.all_gather(lambda_amps, 'col', axis=0, tiled=True)  8.96 us
  transfers between devices with their start and end apart: 2, of which 1 were waited for; matrix products, arithmetic and copies ran while one was open for 28% of the time, Pallas kernels for 0%

commit v1 on v0

v1 whole, which is shorter than its diff:
```python
import functools

import jax
import jax.numpy as jnp
from jax import lax
from jax.experimental import pallas as pl
from jax.experimental.pallas import tpu as pltpu
from jax.sharding import PartitionSpec as P

MESH = pl.DeviceIdType.MESH
LANES = 128
CHUNKS = 8
TILE = 256


def split(value):
    high = value.astype(jnp.bfloat16)
    low = (value - high.astype(jnp.float32)).astype(jnp.bfloat16)
    return high, low


def look_up(table, index):
    row, lane = index // LANES, index % LANES
    found = jnp.zeros(index.shape, table.dtype)
    for t in range(table.shape[0]):
        spread = jnp.broadcast_to(table[t : t + 1, :], index.shape)
        here = jnp.take_along_axis(spread, lane, axis=1, mode="promise_in_bounds")
        found = jnp.where(row == t, here, found)
    return found


def kernel(
    n_row, n_col,
    lam_hbm, inter_hbm, exch_hbm, occ_hbm, virt_hbm, rows_hbm, cols_hbm, out_ref,
    lam, inter, acc, stage, recv, cyc, exch, occ, virt, rows, cols, pair,
    small_sem, own_sem, inter_sem, lam_send, lam_recv, tile_send, tile_recv,
):
    n_dev = n_row * n_col
    my_row, my_col = lax.axis_index("row"), lax.axis_index("col")
    me = my_row * n_col + my_col
    held, depth = lam_hbm.shape
    step = depth // CHUNKS
    width = inter_hbm.shape[1]
    bra = lam.shape[0]
    blocks = width // LANES

    def inter_copy(k):
        return pltpu.make_async_copy(
            inter_hbm.at[pl.ds(pl.multiple_of(k * step, step), step), :], inter.at[k], inter_sem.at[k]
        )

    for k in range(CHUNKS):
        inter_copy(k).start()

    barrier = pltpu.get_barrier_semaphore()

    def greet(k, carry):
        to = lax.rem(me + k, n_dev)
        pl.semaphore_signal(
            barrier, inc=1, device_id=(to // n_col, lax.rem(to, n_col)), device_id_type=MESH
        )
        return carry

    lax.fori_loop(1, n_dev, greet, 0)

    my_rows = pl.ds(pl.multiple_of(my_col * held, held), held)
    own = pltpu.make_async_copy(lam_hbm, lam.at[my_rows, :], own_sem)
    own.start()
    small = [
        pltpu.make_async_copy(src, dst, small_sem.at[s])
        for s, (src, dst) in enumerate(
            [(exch_hbm, exch), (occ_hbm, occ), (virt_hbm, virt), (rows_hbm, rows), (cols_hbm, cols)]
        )
    ]
    for copy in small:
        copy.start()
    pl.semaphore_wait(barrier, n_dev - 1)

    def push(k, carry):
        part = pl.ds(pl.multiple_of(k * step, step), step)
        for d in range(1, n_col):
            pltpu.make_async_remote_copy(
                src_ref=lam_hbm.at[:, part],
                dst_ref=lam.at[my_rows, part],
                send_sem=lam_send,
                recv_sem=lam_recv.at[k],
                device_id=(my_row, lax.rem(my_col + d, n_col)),
                device_id_type=MESH,
            ).start()
        return carry

    lax.fori_loop(0, CHUNKS, push, 0)
    own.wait()
    others = pl.ds(0, (n_col - 1) * held)
    acc[...] = jnp.zeros_like(acc)

    def multiply(k, carry):
        part = pl.ds(pl.multiple_of(k * step, step), step)
        arrived = lam.at[others, part]
        pltpu.make_async_copy(arrived, arrived, lam_recv.at[k]).wait()
        inter_copy(k).wait()
        high, low = split(lam[:, part])
        both = jnp.concatenate([high, low], axis=0)
        for c in range(0, width, TILE):
            at = slice(c, c + TILE)
            inter_high, inter_low = split(inter[k, :, at])
            first = jnp.dot(both, inter_high, preferred_element_type=jnp.float32)
            second = jnp.dot(high, inter_low, preferred_element_type=jnp.float32)
            acc[:, at] += first[:bra] + (first[bra:] + second)
        return carry

    lax.fori_loop(0, CHUNKS, multiply, 0)

    for b in range(blocks):
        stage[:, b, :] = acc[:, b * LANES : (b + 1) * LANES]

    def scatter(k, carry):
        to = lax.rem(me + k, n_dev)
        pltpu.make_async_remote_copy(
            src_ref=stage.at[to],
            dst_ref=recv.at[me],
            send_sem=tile_send,
            recv_sem=tile_recv,
            device_id=(to // n_col, lax.rem(to, n_col)),
            device_id_type=MESH,
        ).start()
        return carry

    lax.fori_loop(1, n_dev, scatter, 0)
    recv[me] = stage[me]

    for copy in small:
        copy.wait()
    lines = cyc.shape[0]
    for q in range(lines):
        for s in range(2):
            pair[s, q : q + 1, :] = cols[s : s + 1, q * LANES : (q + 1) * LANES]
    col_part = look_up(virt[...], pair[0]) + look_up(virt[...], pair[1])
    orbital = jnp.sum(
        jnp.where(lax.broadcasted_iota(jnp.int32, rows.shape, 1) == me, rows[...], 0), axis=1, keepdims=True
    )
    spread = (2, occ.shape[1])
    picked = jnp.sum(
        jnp.where(
            lax.broadcasted_iota(jnp.int32, spread, 1) == orbital, jnp.broadcast_to(occ[...], spread), 0.0
        ),
        axis=1,
        keepdims=True,
    )
    row_part = picked[0:1] + picked[1:2]
    denom = row_part - col_part
    index = exch[...]

    rest = recv.at[pl.ds(0, n_dev - 1)]
    pltpu.make_async_copy(rest, rest, tile_recv).wait()
    total = recv[pl.ds(0, n_col)]
    for i in range(1, n_row):
        total = total + recv[pl.ds(i * n_col, n_col)]
    for j in range(n_col):
        cyc[j * blocks : (j + 1) * blocks, :] = total[j]
    cycle = cyc[...]
    out_ref[...] = (cycle - look_up(cycle, index)) / denom

    sent = stage.at[pl.ds(0, n_dev - 1)]
    pltpu.make_async_copy(sent, sent, tile_send).wait()
    gone = lam.at[others, :]
    pltpu.make_async_copy(gone, gone, lam_send).wait()


def shards(
    lambda_amps, cycle_inter, exchanged, occ_energy, virt_energy, row_orbitals, col_orbitals
):
    n_row, n_col = lax.axis_size("row"), lax.axis_size("col")
    n_dev = n_row * n_col
    held, depth = lambda_amps.shape
    width = cycle_inter.shape[1]
    bra = held * n_col
    window = exchanged.shape[0]
    assert bra == n_dev
    blocks, lines = width // LANES, window // LANES
    f32, i32 = jnp.float32, jnp.int32
    small = [
        exchanged.reshape(lines, LANES),
        occ_energy.reshape(1, -1),
        virt_energy.reshape(-1, LANES),
        row_orbitals.T,
        col_orbitals.T,
    ]
    out = pl.pallas_call(
        functools.partial(kernel, n_row, n_col),
        out_shape=jax.ShapeDtypeStruct((lines, LANES), f32),
        in_specs=[pl.BlockSpec(memory_space=pl.ANY)] * 7,
        out_specs=pl.BlockSpec(memory_space=pltpu.VMEM),
        scratch_shapes=[
            pltpu.VMEM((bra, depth), f32),
            pltpu.VMEM((CHUNKS, depth // CHUNKS, width), f32),
            pltpu.VMEM((bra, width), f32),
            pltpu.VMEM((n_dev, blocks, LANES), f32),
            pltpu.VMEM((n_dev, blocks, LANES), f32),
            pltpu.VMEM((lines, LANES), f32),
            *[pltpu.VMEM(x.shape, x.dtype) for x in small],
            pltpu.VMEM((2, lines, LANES), i32),
            pltpu.SemaphoreType.DMA((5,)),
            pltpu.SemaphoreType.DMA,
            pltpu.SemaphoreType.DMA((CHUNKS,)),
            pltpu.SemaphoreType.DMA,
            pltpu.SemaphoreType.DMA((CHUNKS,)),
            pltpu.SemaphoreType.DMA,
            pltpu.SemaphoreType.DMA,
        ],
        compiler_params=pltpu.CompilerParams(
            collective_id=0, has_side_effects=True, vmem_limit_bytes=56 * 2**20
        ),
        cost_estimate=pl.CostEstimate(
            flops=2 * bra * depth * width, bytes_accessed=4 * depth * width, transcendentals=0
        ),
    )(lambda_amps, cycle_inter, *small)
    return out.reshape(1, window)


def solution(mesh):
    placed = (P("col", "row"), P("row", "col"), P(), P(), P(), P(), P())
    return jax.shard_map(
        shards, mesh=mesh, in_specs=placed, out_specs=P(("row", "col"), None), check_vma=False
    )
```

time: 193 us -> 22.1 us (0.11)
  local copies, waits for them, and re-layouts: 78 us -> 1.32 us
  waiting for transfers between devices: 69.2 us -> 0 us
  Pallas kernels: 0 us -> 20.5 us
  between operations: 19 us -> 0.01 us
  matrix products: 13.8 us -> 0 us
  blocking collectives: 8.96 us -> 0 us
  starting transfers between devices: 3.29 us -> 0 us
    gather x4 -> x0, local copies, waits for them, and re-layouts: 75.4 us -> none  [the longest x1 25.8 us: shards(): jnp.take(virt_energy, col_orbitals[:, 0])]
    unnamed x2 -> x0, waiting for transfers between devices: 69.2 us -> none
    pallas_call x0 -> x1, Pallas kernels: none -> 20.5 us  [shards(): pl.pallas_call(functools.partial(kernel, n_row, n_col), out_shape=jax.Sha...]
    dot_general x1 -> x0, matrix products: 13.8 us -> none  [shards(): jnp.dot(lax.all_gather(lambda_amps, 'col', axis=0, tiled=True), cycle_int...]
    all_gather x1 -> x0, blocking collectives: 8.96 us -> none  [shards(): lax.all_gather(lambda_amps, 'col', axis=0, tiled=True)]
    all_to_all x1 -> x0, starting transfers between devices: 3.25 us -> none  [shards(): lax.all_to_all(summed, 'col', split_axis=0, concat_axis=1, tiled=True)]
  transfers between devices with their start and end apart: 2 -> 0, of which waited for: 1 -> 0; matrix products, arithmetic and copies ran while one was open for 28% -> 0% of each run, Pallas kernels for 0% -> 0%
where the time goes in v1:
time: 22.1 us; the launch traced here: 21.8 us
  Pallas kernels  20.5 us (93%)
  local copies, waits for them, and re-layouts  1.32 us (6%)
    pallas_call x1, Pallas kernels, shards(): pl.pallas_call(functools.partial(kernel, n_row, n_col), out_shape=jax.Sha...  20.5 us
    unnamed x1, local copies, waits for them, and re-layouts  1.32 us

profile of v1, /device:TPU:0, one launch (start us, length us, event | category | flops | bytes accessed | tf_op | source)
XLA Modules:
  0.0 21.8 jit_solution(515367515926874049)
XLA Ops:
  0.0 20.5 %shard_map.73 = f32[32,128]{1,0:T(8,128)} custom-call(f32[8,4096]{1,0:T(8,128)} %lam_hbm.1, f32[4096,1024]{1,0:T(8,128)} %inter_hbm.1, s32[32,128]{1,0:T(8,128)} %bitcast.8, f32[1,64]{1,0:T(1,128)} %bitcast.11, f32[4,128]{1,0:T(4,128)} %bitcast.9, s32[2,32]{1,0:T(2,128)} %bitcast.10, s32[2,4096]{1,0:T(2,128)} %bitcast.7), custom_call_target="tpu_custom_call" | custom-call | flops 268435456 | bytes 16777216 | tf_op jit(solution)/shard_map/pallas_call | solution.py:189
  20.5 1.3 %copy.9 = f32[1,4096]{1,0:T(1,128)} copy(f32[1,4096]{1,0:T(1,128)} %bitcast.6) | data formatting | bytes 32768

commit v2 on v1

--- a/solution.py
+++ b/solution.py
@@ -10,6 +10,7 @@
 MESH = pl.DeviceIdType.MESH
 LANES = 128
 CHUNKS = 8
+AHEAD = 2
 TILE = 256
 
 
@@ -31,9 +32,10 @@
 
 def kernel(
     n_row, n_col,
-    lam_hbm, inter_hbm, exch_hbm, occ_hbm, virt_hbm, rows_hbm, cols_hbm, out_ref,
+    lam_hbm, inter_hbm, exch_hbm, occ_hbm, virt_hbm, rows_hbm, cols_hbm, anti_ref, denom_ref,
     lam, inter, acc, stage, recv, cyc, exch, occ, virt, rows, cols, pair,
-    small_sem, own_sem, inter_sem, lam_send, lam_recv, tile_send, tile_recv,
+    small_sem, own_sem, inter_sem, near_send, near_recv, far_send, far_recv, relay_send, relay_recv,
+    tile_send, tile_recv,
 ):
     n_dev = n_row * n_col
     my_row, my_col = lax.axis_index("row"), lax.axis_index("col")
@@ -76,30 +78,67 @@
         copy.start()
     pl.semaphore_wait(barrier, n_dev - 1)
 
+    def chunk(k):
+        return pl.ds(pl.multiple_of(k * step, step), step)
+
+    def rows_of(col):
+        return pl.ds(pl.multiple_of(col * held, held), held)
+
+    core = lax.rem(my_col, 2)
+    mate = my_col + 1 - 2 * core
+    n_far = n_col // 2 - 1
+    peers = [lax.rem(my_col + 2 * d, n_col) for d in range(1, n_far + 1)]
+
     def push(k, carry):
-        part = pl.ds(pl.multiple_of(k * step, step), step)
-        for d in range(1, n_col):
+        for peer in peers:
             pltpu.make_async_remote_copy(
-                src_ref=lam_hbm.at[:, part],
-                dst_ref=lam.at[my_rows, part],
-                send_sem=lam_send,
-                recv_sem=lam_recv.at[k],
-                device_id=(my_row, lax.rem(my_col + d, n_col)),
+                src_ref=lam_hbm.at[:, chunk(k)],
+                dst_ref=lam.at[my_rows, chunk(k)],
+                send_sem=far_send,
+                recv_sem=far_recv.at[k],
+                device_id=(my_row, peer),
                 device_id_type=MESH,
             ).start()
         return carry
 
+    def forward(k):
+        arrived = lam.at[pl.ds(0, n_far * held), chunk(k)]
+        pltpu.make_async_copy(arrived, arrived, far_recv.at[k]).wait()
+        for peer in peers:
+            pltpu.make_async_remote_copy(
+                src_ref=lam.at[rows_of(peer), chunk(k)],
+                dst_ref=lam.at[rows_of(peer), chunk(k)],
+                send_sem=relay_send,
+                recv_sem=relay_recv.at[k],
+                device_id=(my_row, mate),
+                device_id_type=MESH,
+            ).start()
+
     lax.fori_loop(0, CHUNKS, push, 0)
+    near = pltpu.make_async_remote_copy(
+        src_ref=lam_hbm,
+        dst_ref=lam.at[my_rows, :],
+        send_sem=near_send,
+        recv_sem=near_recv,
+        device_id=(my_row, mate),
+        device_id_type=MESH,
+    )
+    near.start()
+    for k in range(AHEAD):
+        forward(k)
+    near.wait_recv()
     own.wait()
-    others = pl.ds(0, (n_col - 1) * held)
     acc[...] = jnp.zeros_like(acc)
 
     def multiply(k, carry):
-        part = pl.ds(pl.multiple_of(k * step, step), step)
-        arrived = lam.at[others, part]
-        pltpu.make_async_copy(arrived, arrived, lam_recv.at[k]).wait()
+        @pl.when(k + AHEAD < CHUNKS)
+        def _():
+            forward(k + AHEAD)
+
+        arrived = lam.at[pl.ds(0, n_far * held), chunk(k)]
+        pltpu.make_async_copy(arrived, arrived, relay_recv.at[k]).wait()
         inter_copy(k).wait()
-        high, low = split(lam[:, part])
+        high, low = split(lam[:, chunk(k)])
         both = jnp.concatenate([high, low], axis=0)
         for c in range(0, width, TILE):
             at = slice(c, c + TILE)
@@ -148,7 +187,7 @@
         keepdims=True,
     )
     row_part = picked[0:1] + picked[1:2]
-    denom = row_part - col_part
+    denom_ref[...] = row_part - col_part
     index = exch[...]
 
     rest = recv.at[pl.ds(0, n_dev - 1)]
@@ -159,12 +198,14 @@
     for j in range(n_col):
         cyc[j * blocks : (j + 1) * blocks, :] = total[j]
     cycle = cyc[...]
-    out_ref[...] = (cycle - look_up(cycle, index)) / denom
+    anti_ref[...] = cycle - look_up(cycle, index)
 
     sent = stage.at[pl.ds(0, n_dev - 1)]
     pltpu.make_async_copy(sent, sent, tile_send).wait()
-    gone = lam.at[others, :]
-    pltpu.make_async_copy(gone, gone, lam_send).wait()
+    near.wait_send()
+    gone = lam.at[pl.ds(0, n_far * held), :]
+    pltpu.make_async_copy(gone, gone, far_send).wait()
+    pltpu.make_async_copy(gone, gone, relay_send).wait()
 
 
 def shards(
@@ -176,7 +217,7 @@
     width = cycle_inter.shape[1]
     bra = held * n_col
     window = exchanged.shape[0]
-    assert bra == n_dev
+    assert bra == n_dev and n_col % 2 == 0 and n_col > 2
     blocks, lines = width // LANES, window // LANES
     f32, i32 = jnp.float32, jnp.int32
     small = [
@@ -186,11 +227,12 @@
         row_orbitals.T,
         col_orbitals.T,
     ]
-    out = pl.pallas_call(
+    line = jax.ShapeDtypeStruct((lines, LANES), f32)
+    anti, denom = pl.pallas_call(
         functools.partial(kernel, n_row, n_col),
-        out_shape=jax.ShapeDtypeStruct((lines, LANES), f32),
+        out_shape=(line, line),
         in_specs=[pl.BlockSpec(memory_space=pl.ANY)] * 7,
-        out_specs=pl.BlockSpec(memory_space=pltpu.VMEM),
+        out_specs=(pl.BlockSpec(memory_space=pltpu.VMEM),) * 2,
         scratch_shapes=[
             pltpu.VMEM((bra, depth), f32),
             pltpu.VMEM((CHUNKS, depth // CHUNKS, width), f32),
@@ -204,6 +246,10 @@
             pltpu.SemaphoreType.DMA,
             pltpu.SemaphoreType.DMA((CHUNKS,)),
             pltpu.SemaphoreType.DMA,
+            pltpu.SemaphoreType.DMA,
+            pltpu.SemaphoreType.DMA,
+            pltpu.SemaphoreType.DMA((CHUNKS,)),
+            pltpu.SemaphoreType.DMA,
             pltpu.SemaphoreType.DMA((CHUNKS,)),
             pltpu.SemaphoreType.DMA,
             pltpu.SemaphoreType.DMA,
@@ -215,7 +261,7 @@
             flops=2 * bra * depth * width, bytes_accessed=4 * depth * width, transcendentals=0
         ),
     )(lambda_amps, cycle_inter, *small)
-    return out.reshape(1, window)
+    return (anti / denom).reshape(1, window)
 
 
 def solution(mesh):

time: 22.1 us -> 22.1 us (level)
  other arithmetic: 0 us -> 1.35 us
  local copies, waits for them, and re-layouts: 1.32 us -> 0 us
    div x0 -> x1, other arithmetic: none -> 1.35 us  [shards(): return (anti / denom).reshape(1, window)]
    unnamed x1 -> x0, local copies, waits for them, and re-layouts: 1.32 us -> none
where the time goes in v2:
time: 22.1 us; the launch traced here: 21.8 us
  Pallas kernels  20.5 us (93%)
  other arithmetic  1.35 us (6%)
    pallas_call x1, Pallas kernels, shards(): pl.pallas_call(functools.partial(kernel, n_row, n_col), out_shape=(line,...  20.5 us
    div x1, other arithmetic, shards(): return (anti / denom).reshape(1, window)  1.35 us

profile of v2, /device:TPU:0, one launch (start us, length us, event | category | flops | bytes accessed | tf_op | source)
XLA Modules:
  0.0 21.8 jit_solution(14520347107878146104)
XLA Ops:
  0.0 20.5 %shard_map.73 = (f32[32,128]{1,0:T(8,128)}, f32[32,128]{1,0:T(8,128)}) custom-call(f32[8,4096]{1,0:T(8,128)} %lam_hbm.1, f32[4096,1024]{1,0:T(8,128)} %inter_hbm.1, s32[32,128]{1,0:T(8,128)} %bitcast.7, f32[1,64]{1,0:T(1,128)} %bitcast.10, f32[4,128]{1,0:T(4,128)} %bitcast.8, s32[2,32]{1,0:T(2,128)} %bitcast.9, s32[2,4096]{1,0:T(2,128)} %bitcast.6), custom_call_target="tpu_custom_call" | custom-call | flops 268435456 | bytes 16777216 | tf_op jit(solution)/shard_map/pallas_call | solution.py:231
  20.5 1.4 %div.3 = f32[32,128]{1,0:T(8,128)} divide(f32[32,128]{1,0:T(8,128)} %get-tuple-element.7, f32[32,128]{1,0:T(8,128)} %get-tuple-element.8) | non-fusion elementwise | flops 4096 | bytes 49152 | tf_op jit(solution)/shard_map/div | solution.py:264

commit v3 on v2

--- a/solution.py
+++ b/solution.py
@@ -33,11 +33,12 @@
 def kernel(
     n_row, n_col,
     lam_hbm, inter_hbm, exch_hbm, occ_hbm, virt_hbm, rows_hbm, cols_hbm, anti_ref, denom_ref,
-    lam, inter, acc, stage, recv, cyc, exch, occ, virt, rows, cols, pair,
+    lam, inter, even_high, even_low, odd_high, odd_low, acc, stage, recv, cyc, exch, occ, virt, rows, cols, pair,
     small_sem, own_sem, inter_sem, near_send, near_recv, far_send, far_recv, relay_send, relay_recv,
     tile_send, tile_recv,
 ):
     n_dev = n_row * n_col
+    even, odd = (even_high, even_low), (odd_high, odd_low)
     my_row, my_col = lax.axis_index("row"), lax.axis_index("col")
     me = my_row * n_col + my_col
     held, depth = lam_hbm.shape
@@ -124,31 +125,49 @@
         device_id_type=MESH,
     )
     near.start()
+    acc[...] = jnp.zeros_like(acc)
+
+    tiles = [(r, c) for c in range(0, width, TILE) for r in range(0, step, TILE)]
+
+    def convert(k, part, r, c):
+        at = (slice(r, r + TILE), slice(c, c + TILE))
+        part[0][at], part[1][at] = split(inter[k, at[0], at[1]])
+
+    def multiply(k, ready, filling):
+        @pl.when(k + AHEAD < CHUNKS)
+        def _():
+            forward(k + AHEAD)
+
+        @pl.when(k + 1 < CHUNKS)
+        def _():
+            inter_copy(k + 1).wait()
+
+        arrived = lam.at[pl.ds(0, n_far * held), chunk(k)]
+        pltpu.make_async_copy(arrived, arrived, relay_recv.at[k]).wait()
+        after = jnp.minimum(k + 1, CHUNKS - 1)
+        high, low = split(lam[:, chunk(k)])
+        both = jnp.concatenate([high, low], axis=0)
+        for r, c in tiles:
+            convert(after, filling, r, c)
+            rows_at, at = slice(r, r + TILE), slice(c, c + TILE)
+            first = jnp.dot(both[:, rows_at], ready[0][rows_at, at], preferred_element_type=jnp.float32)
+            second = jnp.dot(high[:, rows_at], ready[1][rows_at, at], preferred_element_type=jnp.float32)
+            acc[:, at] += first[:bra] + (first[bra:] + second)
+
+    inter_copy(0).wait()
+    for r, c in tiles:
+        convert(0, even, r, c)
     for k in range(AHEAD):
         forward(k)
     near.wait_recv()
     own.wait()
-    acc[...] = jnp.zeros_like(acc)
-
-    def multiply(k, carry):
-        @pl.when(k + AHEAD < CHUNKS)
-        def _():
-            forward(k + AHEAD)
-
-        arrived = lam.at[pl.ds(0, n_far * held), chunk(k)]
-        pltpu.make_async_copy(arrived, arrived, relay_recv.at[k]).wait()
-        inter_copy(k).wait()
-        high, low = split(lam[:, chunk(k)])
-        both = jnp.concatenate([high, low], axis=0)
-        for c in range(0, width, TILE):
-            at = slice(c, c + TILE)
-            inter_high, inter_low = split(inter[k, :, at])
-            first = jnp.dot(both, inter_high, preferred_element_type=jnp.float32)
-            second = jnp.dot(high, inter_low, preferred_element_type=jnp.float32)
-            acc[:, at] += first[:bra] + (first[bra:] + second)
-        return carry
-
-    lax.fori_loop(0, CHUNKS, multiply, 0)
+
+    def twice(t, carry):
+        multiply(2 * t, even, odd)
+        multiply(2 * t + 1, odd, even)
+        return carry
+
+    lax.fori_loop(0, CHUNKS // 2, twice, 0)
 
     for b in range(blocks):
         stage[:, b, :] = acc[:, b * LANES : (b + 1) * LANES]
@@ -236,6 +255,7 @@
         scratch_shapes=[
             pltpu.VMEM((bra, depth), f32),
             pltpu.VMEM((CHUNKS, depth // CHUNKS, width), f32),
+            *[pltpu.VMEM((depth // CHUNKS, width), jnp.bfloat16)] * 4,
             pltpu.VMEM((bra, width), f32),
             pltpu.VMEM((n_dev, blocks, LANES), f32),
             pltpu.VMEM((n_dev, blocks, LANES), f32),

time: 22.1 us -> 26 us (1.18)
  Pallas kernels: 20.5 us -> 24.4 us
    pallas_call x1, Pallas kernels: 20.5 us -> 24.4 us  [shards(): pl.pallas_call(functools.partial(kernel, n_row, n_col), out_shape=(line,...]
where the time goes in v3:
time: 26 us; the launch traced here: 25.8 us
  Pallas kernels  24.4 us (94%)
  other arithmetic  1.35 us (5%)
    pallas_call x1, Pallas kernels, shards(): pl.pallas_call(functools.partial(kernel, n_row, n_col), out_shape=(line,...  24.4 us
    div x1, other arithmetic, shards(): return (anti / denom).reshape(1, window)  1.35 us

profile of v3, /device:TPU:0, one launch (start us, length us, event | category | flops | bytes accessed | tf_op | source)
XLA Modules:
  0.0 25.8 jit_solution(17395673126695783850)
XLA Ops:
  0.0 24.4 %shard_map.73 = (f32[32,128]{1,0:T(8,128)}, f32[32,128]{1,0:T(8,128)}) custom-call(f32[8,4096]{1,0:T(8,128)} %lam_hbm.1, f32[4096,1024]{1,0:T(8,128)} %inter_hbm.1, s32[32,128]{1,0:T(8,128)} %bitcast.7, f32[1,64]{1,0:T(1,128)} %bitcast.10, f32[4,128]{1,0:T(4,128)} %bitcast.8, s32[2,32]{1,0:T(2,128)} %bitcast.9, s32[2,4096]{1,0:T(2,128)} %bitcast.6), custom_call_target="tpu_custom_call" | custom-call | flops 268435456 | bytes 16777216 | tf_op jit(solution)/shard_map/pallas_call | solution.py:250
  24.4 1.4 %div.3 = f32[32,128]{1,0:T(8,128)} divide(f32[32,128]{1,0:T(8,128)} %get-tuple-element.7, f32[32,128]{1,0:T(8,128)} %get-tuple-element.8) | non-fusion elementwise | flops 4096 | bytes 49152 | tf_op jit(solution)/shard_map/div | solution.py:284

commit v4 on v2

--- a/solution.py
+++ b/solution.py
@@ -9,8 +9,8 @@
 
 MESH = pl.DeviceIdType.MESH
 LANES = 128
-CHUNKS = 8
-AHEAD = 2
+CHUNKS = 4
+AHEAD = 1
 TILE = 256
 
 
@@ -142,9 +142,12 @@
         both = jnp.concatenate([high, low], axis=0)
         for c in range(0, width, TILE):
             at = slice(c, c + TILE)
-            inter_high, inter_low = split(inter[k, :, at])
-            first = jnp.dot(both, inter_high, preferred_element_type=jnp.float32)
-            second = jnp.dot(high, inter_low, preferred_element_type=jnp.float32)
+            first = second = 0.0
+            for r in range(0, step, TILE):
+                rows_at = slice(r, r + TILE)
+                inter_high, inter_low = split(inter[k, rows_at, at])
+                first += jnp.dot(both[:, rows_at], inter_high, preferred_element_type=jnp.float32)
+                second += jnp.dot(high[:, rows_at], inter_low, preferred_element_type=jnp.float32)
             acc[:, at] += first[:bra] + (first[bra:] + second)
         return carry
 

time: 22.1 us -> 21.7 us (0.982)
  Pallas kernels: 20.5 us -> 20.1 us
    pallas_call x1, Pallas kernels: 20.5 us -> 20.1 us  [shards(): pl.pallas_call(functools.partial(kernel, n_row, n_col), out_shape=(line,...]
where the time goes in v4:
time: 21.7 us; the launch traced here: 21.4 us
  Pallas kernels  20.1 us (93%)
  other arithmetic  1.35 us (6%)
    pallas_call x1, Pallas kernels, shards(): pl.pallas_call(functools.partial(kernel, n_row, n_col), out_shape=(line,...  20.1 us
    div x1, other arithmetic, shards(): return (anti / denom).reshape(1, window)  1.35 us

profile of v4, /device:TPU:0, one launch (start us, length us, event | category | flops | bytes accessed | tf_op | source)
XLA Modules:
  0.0 21.4 jit_solution(7242845182958964301)
XLA Ops:
  0.0 20.1 %shard_map.73 = (f32[32,128]{1,0:T(8,128)}, f32[32,128]{1,0:T(8,128)}) custom-call(f32[8,4096]{1,0:T(8,128)} %lam_hbm.1, f32[4096,1024]{1,0:T(8,128)} %inter_hbm.1, s32[32,128]{1,0:T(8,128)} %bitcast.7, f32[1,64]{1,0:T(1,128)} %bitcast.10, f32[4,128]{1,0:T(4,128)} %bitcast.8, s32[2,32]{1,0:T(2,128)} %bitcast.9, s32[2,4096]{1,0:T(2,128)} %bitcast.6), custom_call_target="tpu_custom_call" | custom-call | flops 268435456 | bytes 16777216 | tf_op jit(solution)/shard_map/pallas_call | solution.py:234
  20.1 1.4 %div.3 = f32[32,128]{1,0:T(8,128)} divide(f32[32,128]{1,0:T(8,128)} %get-tuple-element.7, f32[32,128]{1,0:T(8,128)} %get-tuple-element.8) | non-fusion elementwise | flops 4096 | bytes 49152 | tf_op jit(solution)/shard_map/div | solution.py:267

commit v5 on v4

--- a/solution.py
+++ b/solution.py
@@ -33,9 +33,9 @@
 def kernel(
     n_row, n_col,
     lam_hbm, inter_hbm, exch_hbm, occ_hbm, virt_hbm, rows_hbm, cols_hbm, anti_ref, denom_ref,
-    lam, inter, acc, stage, recv, cyc, exch, occ, virt, rows, cols, pair,
+    lam, inter, acc, stage, recv, summed, whole, cyc, exch, occ, virt, rows, cols, pair,
     small_sem, own_sem, inter_sem, near_send, near_recv, far_send, far_recv, relay_send, relay_recv,
-    tile_send, tile_recv,
+    tile_send, tile_recv, row_send, row_recv,
 ):
     n_dev = n_row * n_col
     my_row, my_col = lax.axis_index("row"), lax.axis_index("col")
@@ -56,14 +56,17 @@
 
     barrier = pltpu.get_barrier_semaphore()
 
-    def greet(k, carry):
-        to = lax.rem(me + k, n_dev)
+    def greet_row(k, carry):
         pl.semaphore_signal(
-            barrier, inc=1, device_id=(to // n_col, lax.rem(to, n_col)), device_id_type=MESH
+            barrier, inc=1, device_id=(lax.rem(my_row + k, n_row), my_col), device_id_type=MESH
         )
         return carry
 
-    lax.fori_loop(1, n_dev, greet, 0)
+    for d in range(1, n_col):
+        pl.semaphore_signal(
+            barrier, inc=1, device_id=(my_row, lax.rem(my_col + d, n_col)), device_id_type=MESH
+        )
+    lax.fori_loop(1, n_row, greet_row, 0)
 
     my_rows = pl.ds(pl.multiple_of(my_col * held, held), held)
     own = pltpu.make_async_copy(lam_hbm, lam.at[my_rows, :], own_sem)
@@ -76,7 +79,7 @@
     ]
     for copy in small:
         copy.start()
-    pl.semaphore_wait(barrier, n_dev - 1)
+    pl.semaphore_wait(barrier, n_row + n_col - 2)
 
     def chunk(k):
         return pl.ds(pl.multiple_of(k * step, step), step)
@@ -156,20 +159,23 @@
     for b in range(blocks):
         stage[:, b, :] = acc[:, b * LANES : (b + 1) * LANES]
 
+    def group(row):
+        return pl.ds(row * n_col, n_col)
+
     def scatter(k, carry):
-        to = lax.rem(me + k, n_dev)
+        to = lax.rem(my_row + k, n_row)
         pltpu.make_async_remote_copy(
-            src_ref=stage.at[to],
-            dst_ref=recv.at[me],
+            src_ref=stage.at[group(to)],
+            dst_ref=recv.at[group(my_row)],
             send_sem=tile_send,
             recv_sem=tile_recv,
-            device_id=(to // n_col, lax.rem(to, n_col)),
+            device_id=(to, my_col),
             device_id_type=MESH,
         ).start()
         return carry
 
-    lax.fori_loop(1, n_dev, scatter, 0)
-    recv[me] = stage[me]
+    lax.fori_loop(1, n_row, scatter, 0)
+    recv[group(my_row)] = stage[group(my_row)]
 
     for copy in small:
         copy.wait()
@@ -193,18 +199,35 @@
     denom_ref[...] = row_part - col_part
     index = exch[...]
 
-    rest = recv.at[pl.ds(0, n_dev - 1)]
+    rest = recv.at[pl.ds(0, n_dev - n_col)]
     pltpu.make_async_copy(rest, rest, tile_recv).wait()
     total = recv[pl.ds(0, n_col)]
     for i in range(1, n_row):
         total = total + recv[pl.ds(i * n_col, n_col)]
+    summed[...] = total
+
+    for d in range(1, n_col):
+        to = lax.rem(my_col + d, n_col)
+        pltpu.make_async_remote_copy(
+            src_ref=summed.at[to],
+            dst_ref=whole.at[my_col],
+            send_sem=row_send,
+            recv_sem=row_recv,
+            device_id=(my_row, to),
+            device_id_type=MESH,
+        ).start()
+    whole[my_col] = summed[my_col]
+    rest = whole.at[pl.ds(0, n_col - 1)]
+    pltpu.make_async_copy(rest, rest, row_recv).wait()
     for j in range(n_col):
-        cyc[j * blocks : (j + 1) * blocks, :] = total[j]
+        cyc[j * blocks : (j + 1) * blocks, :] = whole[j]
     cycle = cyc[...]
     anti_ref[...] = cycle - look_up(cycle, index)
 
-    sent = stage.at[pl.ds(0, n_dev - 1)]
+    sent = stage.at[pl.ds(0, n_dev - n_col)]
     pltpu.make_async_copy(sent, sent, tile_send).wait()
+    sent = summed.at[pl.ds(0, n_col - 1)]
+    pltpu.make_async_copy(sent, sent, row_send).wait()
     near.wait_send()
     gone = lam.at[pl.ds(0, n_far * held), :]
     pltpu.make_async_copy(gone, gone, far_send).wait()
@@ -242,6 +265,8 @@
             pltpu.VMEM((bra, width), f32),
             pltpu.VMEM((n_dev, blocks, LANES), f32),
             pltpu.VMEM((n_dev, blocks, LANES), f32),
+            pltpu.VMEM((n_col, blocks, LANES), f32),
+            pltpu.VMEM((n_col, blocks, LANES), f32),
             pltpu.VMEM((lines, LANES), f32),
             *[pltpu.VMEM(x.shape, x.dtype) for x in small],
             pltpu.VMEM((2, lines, LANES), i32),
@@ -254,6 +279,8 @@
             pltpu.SemaphoreType.DMA((CHUNKS,)),
             pltpu.SemaphoreType.DMA,
             pltpu.SemaphoreType.DMA((CHUNKS,)),
+            pltpu.SemaphoreType.DMA,
+            pltpu.SemaphoreType.DMA,
             pltpu.SemaphoreType.DMA,
             pltpu.SemaphoreType.DMA,
         ],

time: 21.7 us -> 23.4 us (1.078)
  Pallas kernels: 20.1 us -> 21.8 us
    pallas_call x1, Pallas kernels: 20.1 us -> 21.8 us  [shards(): pl.pallas_call(functools.partial(kernel, n_row, n_col), out_shape=(line,...]
where the time goes in v5:
time: 23.4 us; the launch traced here: 23.1 us
  Pallas kernels  21.8 us (93%)
  other arithmetic  1.35 us (6%)
    pallas_call x1, Pallas kernels, shards(): pl.pallas_call(functools.partial(kernel, n_row, n_col), out_shape=(line,...  21.8 us
    div x1, other arithmetic, shards(): return (anti / denom).reshape(1, window)  1.35 us

profile of v5, /device:TPU:0, one launch (start us, length us, event | category | flops | bytes accessed | tf_op | source)
XLA Modules:
  0.0 23.1 jit_solution(17773833799449978685)
XLA Ops:
  0.0 21.8 %shard_map.73 = (f32[32,128]{1,0:T(8,128)}, f32[32,128]{1,0:T(8,128)}) custom-call(f32[8,4096]{1,0:T(8,128)} %lam_hbm.1, f32[4096,1024]{1,0:T(8,128)} %inter_hbm.1, s32[32,128]{1,0:T(8,128)} %bitcast.7, f32[1,64]{1,0:T(1,128)} %bitcast.10, f32[4,128]{1,0:T(4,128)} %bitcast.8, s32[2,32]{1,0:T(2,128)} %bitcast.9, s32[2,4096]{1,0:T(2,128)} %bitcast.6), custom_call_target="tpu_custom_call" | custom-call | flops 268435456 | bytes 16777216 | tf_op jit(solution)/shard_map/pallas_call | solution.py:257
  21.8 1.4 %div.3 = f32[32,128]{1,0:T(8,128)} divide(f32[32,128]{1,0:T(8,128)} %get-tuple-element.7, f32[32,128]{1,0:T(8,128)} %get-tuple-element.8) | non-fusion elementwise | flops 4096 | bytes 49152 | tf_op jit(solution)/shard_map/div | solution.py:294

commit v6 on v4

--- a/solution.py
+++ b/solution.py
@@ -46,24 +46,31 @@
     bra = lam.shape[0]
     blocks = width // LANES
 
+    def chunk(k):
+        return pl.ds(k * step if isinstance(k, int) else pl.multiple_of(k * step, step), step)
+
     def inter_copy(k):
         return pltpu.make_async_copy(
-            inter_hbm.at[pl.ds(pl.multiple_of(k * step, step), step), :], inter.at[k], inter_sem.at[k]
+            inter_hbm.at[chunk(k), :], inter.at[k], inter_sem.at[k]
         )
+
+    barrier = pltpu.get_barrier_semaphore()
+
+    columns = [my_col] + [lax.rem(my_col + d, n_col) for d in range(1, n_col)]
+
+    def greet(row, cols_of):
+        for col in cols_of:
+            pl.semaphore_signal(barrier, inc=1, device_id=(row, col), device_id_type=MESH)
+
+    def greet_row(k, carry):
+        greet(lax.rem(my_row + k, n_row), columns)
+        return carry
+
+    lax.fori_loop(1, n_row, greet_row, 0)
+    greet(my_row, columns[1:])
 
     for k in range(CHUNKS):
         inter_copy(k).start()
-
-    barrier = pltpu.get_barrier_semaphore()
-
-    def greet(k, carry):
-        to = lax.rem(me + k, n_dev)
-        pl.semaphore_signal(
-            barrier, inc=1, device_id=(to // n_col, lax.rem(to, n_col)), device_id_type=MESH
-        )
-        return carry
-
-    lax.fori_loop(1, n_dev, greet, 0)
 
     my_rows = pl.ds(pl.multiple_of(my_col * held, held), held)
     own = pltpu.make_async_copy(lam_hbm, lam.at[my_rows, :], own_sem)
@@ -78,9 +85,6 @@
         copy.start()
     pl.semaphore_wait(barrier, n_dev - 1)
 
-    def chunk(k):
-        return pl.ds(pl.multiple_of(k * step, step), step)
-
     def rows_of(col):
         return pl.ds(pl.multiple_of(col * held, held), held)
 
@@ -89,7 +93,7 @@
     n_far = n_col // 2 - 1
     peers = [lax.rem(my_col + 2 * d, n_col) for d in range(1, n_far + 1)]
 
-    def push(k, carry):
+    def push(k):
         for peer in peers:
             pltpu.make_async_remote_copy(
                 src_ref=lam_hbm.at[:, chunk(k)],
@@ -99,7 +103,6 @@
                 device_id=(my_row, peer),
                 device_id_type=MESH,
             ).start()
-        return carry
 
     def forward(k):
         arrived = lam.at[pl.ds(0, n_far * held), chunk(k)]
@@ -114,7 +117,8 @@
                 device_id_type=MESH,
             ).start()
 
-    lax.fori_loop(0, CHUNKS, push, 0)
+    for k in range(CHUNKS):
+        push(k)
     near = pltpu.make_async_remote_copy(
         src_ref=lam_hbm,
         dst_ref=lam.at[my_rows, :],
@@ -156,19 +160,23 @@
     for b in range(blocks):
         stage[:, b, :] = acc[:, b * LANES : (b + 1) * LANES]
 
-    def scatter(k, carry):
-        to = lax.rem(me + k, n_dev)
-        pltpu.make_async_remote_copy(
-            src_ref=stage.at[to],
-            dst_ref=recv.at[me],
-            send_sem=tile_send,
-            recv_sem=tile_recv,
-            device_id=(to // n_col, lax.rem(to, n_col)),
-            device_id_type=MESH,
-        ).start()
+    def scatter(row, cols_of):
+        for col in cols_of:
+            pltpu.make_async_remote_copy(
+                src_ref=stage.at[row * n_col + col],
+                dst_ref=recv.at[me],
+                send_sem=tile_send,
+                recv_sem=tile_recv,
+                device_id=(row, col),
+                device_id_type=MESH,
+            ).start()
+
+    def scatter_row(k, carry):
+        scatter(lax.rem(my_row + k, n_row), columns)
         return carry
 
-    lax.fori_loop(1, n_dev, scatter, 0)
+    lax.fori_loop(1, n_row, scatter_row, 0)
+    scatter(my_row, columns[1:])
     recv[me] = stage[me]
 
     for copy in small:

time: 21.7 us -> 21.7 us (level)
  no operation moved by 1% of the time
where the time goes in v6:
time: 21.7 us; the launch traced here: 21.5 us
  Pallas kernels  20.1 us (93%)
  other arithmetic  1.35 us (6%)
    pallas_call x1, Pallas kernels, shards(): pl.pallas_call(functools.partial(kernel, n_row, n_col), out_shape=(line,...  20.1 us
    div x1, other arithmetic, shards(): return (anti / denom).reshape(1, window)  1.35 us

profile of v6, /device:TPU:0, one launch (start us, length us, event | category | flops | bytes accessed | tf_op | source)
XLA Modules:
  0.0 21.5 jit_solution(14098623446077362383)
XLA Ops:
  0.0 20.1 %shard_map.73 = (f32[32,128]{1,0:T(8,128)}, f32[32,128]{1,0:T(8,128)}) custom-call(f32[8,4096]{1,0:T(8,128)} %lam_hbm.1, f32[4096,1024]{1,0:T(8,128)} %inter_hbm.1, s32[32,128]{1,0:T(8,128)} %bitcast.7, f32[1,64]{1,0:T(1,128)} %bitcast.10, f32[4,128]{1,0:T(4,128)} %bitcast.8, s32[2,32]{1,0:T(2,128)} %bitcast.9, s32[2,4096]{1,0:T(2,128)} %bitcast.6), custom_call_target="tpu_custom_call" | custom-call | flops 268435456 | bytes 16777216 | tf_op jit(solution)/shard_map/pallas_call | solution.py:242
  20.1 1.4 %div.3 = f32[32,128]{1,0:T(8,128)} divide(f32[32,128]{1,0:T(8,128)} %get-tuple-element.7, f32[32,128]{1,0:T(8,128)} %get-tuple-element.8) | non-fusion elementwise | flops 4096 | bytes 49152 | tf_op jit(solution)/shard_map/div | solution.py:275
